TPU v7x, 32 devices: a whole 2x2x4 slice. The times are simulated.
32 devices in a mesh: sec: 2 (over x), sx: 2 (over y), sy: 8 (over z, core).
Axes of the slice: x: 2, y: 2, z: 4, core: 2. Of those that a mesh axis runs over, the one named last changes fastest.
Arguments:
- replay: bfloat16 [2, 8, 32, 2, 8, 256], P('sec', 'sx', 'sy'), may hold values from -6 to 6
- replay_pick: int32 [2, 8, 32], P('sec', 'sx', 'sy'), may hold values from 0 to 1
- w_in: bfloat16 [256, 512], replicated, may hold values from -0.375 to 0.375
- b_in: float32 [512], replicated, may hold values from -3 to 3
- w_out: bfloat16 [512, 8], replicated, may hold values from -0.25 to 0.25
- b_out: float32 [8], replicated, may hold values from -3 to 3
- block_rows: float32 [2, 8, 32, 64, 256], P('sec', 'sx', 'sy'), may hold values from -1.1 to 9.1
- loads: bfloat16 [2, 8, 32, 64, 128], P('sec', 'sx', 'sy'), may hold values from -36 to 36
- fixed_mask: int32 [2, 8, 32, 64], P('sec', 'sx', 'sy'), may hold values 0 or 1
- elem_map: int32 [2, 8, 32], P('sec', 'sx', 'sy'), may hold values from 0 to 31, each once within a row
- cotangent: bfloat16 [2, 8, 32, 64, 128], P('sec', 'sx', 'sy'), may hold values from -0.029907227 to 0.029907227
Outputs:
- solution: float32 [2, 8, 32, 64, 128], P('sec', 'sx', 'sy')
- w_in_grad: float32 [256, 512], replicated
- b_in_grad: float32 [512], replicated
- w_out_grad: float32 [512, 8], replicated
- b_out_grad: float32 [8], replicated
Inputs may be any that keep to these rules, and one draw needn't show every extreme that they name: Each row elem_map[s, x, :] is a permutation of 0 to 31.
All inputs are finite; a program needn't handle non-finite values. No bound on the sum of `fixed_mask` on one device may be relied on, other than what follows from the above.
Results may differ from a plain program's by a relative error of at most 0.0047.
Values sent between devices are 32-bit elements; how exact they have to be, the bound alone decides.
A program may use at most 64 MiB of HBM per device.

v0:
```python
import functools

import jax
import jax.numpy as jnp
from jax import lax
from jax.experimental import pallas as pl
from jax.experimental.pallas import tpu as pltpu
from jax.sharding import PartitionSpec as P

SWEEPS = 4
RELAXATION = 0.8
F32 = jnp.float32
BF16 = jnp.bfloat16
MESH = pl.DeviceIdType.MESH


def mm(a, b):
    return jnp.dot(a, b, preferred_element_type=F32)


def mm_nt(a, b):
    return lax.dot_general(a, b, (((1,), (1,)), ((), ())), preferred_element_type=F32)


def split(v):
    hi = v.astype(BF16)
    lo = (v - hi.astype(F32)).astype(BF16)
    return hi, lo


def mul3(m3, v):
    hi, lo = split(v)
    return mm(m3, jnp.concatenate([hi, hi, lo], axis=0))


def put3(ref, bx, by, m):
    d = m.shape[0]
    hi, lo = split(m)
    ref[bx, by, :, 0:d] = hi
    ref[bx, by, :, d : 2 * d] = lo
    ref[bx, by, :, 2 * d : 3 * d] = hi


def kernel(
    n_sx, n_sy, picked_ref, w_in_ref, b_in_ref, wt_ref, b_out_ref, rows_ref, loads_ref, mask_ref, map_ref,
    cot_ref, u_ref, wg_ref, ex_ref,
    pre, hid, pick_t, gate, own, gath, placed, back, oh, kh_w, kh_s, cm, kd3, kdt3, p3, pt3, mw, cw, rc,
    x_st, h_w, h_e, h_s, h_n, xb, tt, ku, gh, acc_hi, acc_lo,
    sg, rg, sk, rk, s_we, r_we, s_ns, r_ns, sc, rcs,
):
    bx, by, dof = rows_ref.shape[0], rows_ref.shape[1], rows_ref.shape[2]
    groups = bx * by
    lanes = loads_ref.shape[3]
    sec, sx, sy = lax.axis_index("sec"), lax.axis_index("sx"), lax.axis_index("sy")
    has_w, has_e, has_s, has_n = sy > 0, sy < n_sy - 1, sx > 0, sx < n_sx - 1
    west, east = (sec, sx, sy - 1), (sec, sx, sy + 1)
    south, north = (sec, sx - 1, sy), (sec, sx + 1, sy)

    barrier = pltpu.get_barrier_semaphore()
    for k in range(n_sy):
        pl.semaphore_signal(
            barrier, inc=1, device_id=(1 - sec, sx, lax.rem(sy + k, n_sy)), device_id_type=MESH
        )
    for has, dev in ((has_w, west), (has_e, east), (has_s, south), (has_n, north)):

        @pl.when(has)
        def _():
            pl.semaphore_signal(barrier, inc=1, device_id=dev, device_id_type=MESH)

    pre_in = mm(picked_ref[...], w_in_ref[...]) + b_in_ref[...]
    pre[...] = pre_in
    hidden = (pre_in * jax.nn.sigmoid(pre_in)).astype(BF16)
    hid[...] = hidden
    n_rows = hidden.shape[0]
    full = jax.nn.sigmoid(mm_nt(hidden, wt_ref[...]) + b_out_ref[...])
    elem = n_rows // groups
    width = dof // elem
    wide = full.shape[1]
    row_id = lax.broadcasted_iota(jnp.int32, (n_rows, wide), 0)
    col_id = lax.broadcasted_iota(jnp.int32, (n_rows, wide), 1)
    mine = (row_id % elem) == (col_id // width)
    gate_rows = jnp.sum(jnp.where(mine, full, 0.0).reshape(groups, elem, wide), axis=1)
    gate[...] = gate_rows
    own[...] = 0.5 + 2.0 * gate_rows

    one = lambda has: jnp.where(has, 1, 0)
    pl.semaphore_wait(barrier, n_sy + one(has_w) + one(has_e) + one(has_s) + one(has_n))

    def group_copy(k):
        j = lax.rem(sy + k, n_sy)
        return pltpu.make_async_remote_copy(
            src_ref=own, dst_ref=gath.at[sy], send_sem=sg.at[k], recv_sem=rg.at[sy],
            device_id=(1 - sec, sx, j), device_id_type=MESH,
        )

    for k in range(n_sy):
        group_copy(k).start()

    def kw_copy():
        return pltpu.make_async_remote_copy(
            src_ref=rows_ref.at[:, by - 1, :, pl.ds(0, 2 * dof)], dst_ref=kh_w,
            send_sem=sk.at[0], recv_sem=rk.at[0], device_id=east, device_id_type=MESH,
        )

    def ks_copy():
        return pltpu.make_async_remote_copy(
            src_ref=rows_ref.at[bx - 1, :, :, pl.ds(2 * dof, 2 * dof)], dst_ref=kh_s,
            send_sem=sk.at[1], recv_sem=rk.at[1], device_id=north, device_id_type=MESH,
        )

    @pl.when(has_e)
    def _():
        kw_copy().start()

    @pl.when(has_n)
    def _():
        ks_copy().start()

    zero_block = jnp.zeros((dof, dof), BF16)
    for x in range(bx):
        for y in range(by):
            block = rows_ref[x, y]
            turned = block.T
            cm[x, y, :, 0 : 2 * dof] = block[:, dof : 3 * dof].astype(BF16)
            put3(kd3, x, y, block[:, 0:dof])
            put3(p3, x, y, block[:, 3 * dof : 4 * dof])
            put3(kdt3, x, y, turned[0:dof])
            put3(pt3, x, y, turned[3 * dof : 4 * dof])
            if y + 1 < by:
                cm[x, y + 1, :, 2 * dof : 3 * dof] = turned[dof : 2 * dof].astype(BF16)
            if x + 1 < bx:
                cm[x + 1, y, :, 3 * dof : 4 * dof] = turned[2 * dof : 3 * dof].astype(BF16)
            mw[x, y] = jnp.broadcast_to(mask_ref[:, x * by + y : x * by + y + 1], (dof, lanes))
    pick_t[...] = picked_ref[...].astype(F32).T.astype(BF16)
    xb[...] = jnp.zeros_like(xb)

    span = n_sy * groups
    ids = lax.broadcasted_iota(jnp.int32, (span, lanes), 0)
    gid = (ids // groups) * by + ids % by
    gx = (ids // by) % bx
    for x in range(bx):
        for y in range(by):
            b = x * by + y
            hit = (gid == map_ref[x, y]) & (gx == x)
            oh[:, b * lanes : (b + 1) * lanes] = jnp.where(hit, 1.0, 0.0).astype(BF16)

    for j in range(n_sy):
        pltpu.make_async_remote_copy(
            src_ref=own, dst_ref=gath.at[j], send_sem=sg.at[j], recv_sem=rg.at[j],
            device_id=(1 - sec, sx, j), device_id_type=MESH,
        ).wait_recv()
    turned_rows = gath[...].reshape(span, wide).T[0:dof]
    g_hi, g_lo = split(turned_rows)
    for x in range(bx):
        part = oh[:, x * by * lanes : (x + 1) * by * lanes]
        coefs = mm(g_hi, part) + mm(g_lo, part)
        for y in range(by):
            c = coefs[:, y * lanes : (y + 1) * lanes]
            rc[x, y] = 1.0 / c

    def face(direction, r, x):
        if direction == 0:
            return pltpu.make_async_remote_copy(
                src_ref=x_st.at[r, x, 0], dst_ref=h_e.at[r, x], send_sem=s_we.at[0, r, x],
                recv_sem=r_we.at[0, r, x], device_id=west, device_id_type=MESH,
            )
        if direction == 1:
            return pltpu.make_async_remote_copy(
                src_ref=x_st.at[r, x, by - 1], dst_ref=h_w.at[r, x], send_sem=s_we.at[1, r, x],
                recv_sem=r_we.at[1, r, x], device_id=east, device_id_type=MESH,
            )
        if direction == 2:
            return pltpu.make_async_remote_copy(
                src_ref=x_st.at[r, 0], dst_ref=h_n.at[r], send_sem=s_ns.at[0, r],
                recv_sem=r_ns.at[0, r], device_id=south, device_id_type=MESH,
            )
        return pltpu.make_async_remote_copy(
            src_ref=x_st.at[r, bx - 1], dst_ref=h_s.at[r], send_sem=s_ns.at[1, r],
            recv_sem=r_ns.at[1, r], device_id=north, device_id_type=MESH,
        )

    def send_row(r, x):
        @pl.when((r < SWEEPS - 1) & (x == bx - 1) & has_n)
        def _():
            face(3, r, x).start()

        @pl.when((r < SWEEPS - 1) & (x == 0) & has_s)
        def _():
            face(2, r, x).start()

        @pl.when((r < SWEEPS - 1) & has_w)
        def _():
            face(0, r, x).start()

        @pl.when((r < SWEEPS - 1) & has_e)
        def _():
            face(1, r, x).start()

    def row_at(k):
        return jnp.where(sx == 0, k, bx - 1 - k)

    def finish(r, x, y, u, h):
        m = mw[x, y]
        p = RELAXATION * mul3(pt3[x, y], h)
        w = p * rc[x, y]
        x_st[r, x, y, :, 0:lanes] = u
        x_st[r, x, y, :, lanes : 2 * lanes] = w
        slot = lax.rem(r, 2)
        xb[slot, x + 1, y + 1, :, 0:lanes] = u.astype(BF16)
        xb[slot, x + 1, y + 1, :, lanes : 2 * lanes] = w.astype(BF16)
        u_ref[x, y] = u
        gh[x, y] = h
        cw[x, y] = p

    def after(x):
        for y in range(by):
            gh[x, y] = gh[x, y] - mul3(kdt3[x, y], cw[x, y])
            ku[x, y] = mul3(kd3[x, y], u_ref[x, y])

    def first_row(k, _):
        x = row_at(k)
        for y in range(by):
            t = loads_ref[x, y].astype(F32) * rc[x, y]
            tt[0, x, y] = t
            u = mw[x, y] * (RELAXATION * mul3(p3[x, y], t))
            finish(0, x, y, u, mw[x, y] * cot_ref[x, y].astype(F32))
        send_row(0, x)
        after(x)
        return 0

    lax.fori_loop(0, bx, first_row, 0)

    @pl.when(has_w)
    def _():
        kw_copy().wait_recv()
        for x in range(bx):
            cm[x, 0, :, 2 * dof : 3 * dof] = kh_w[x].T[dof : 2 * dof].astype(BF16)

    @pl.when(jnp.logical_not(has_w))
    def _():
        for x in range(bx):
            cm[x, 0, :, 2 * dof : 3 * dof] = zero_block

    @pl.when(has_s)
    def _():
        ks_copy().wait_recv()
        for y in range(by):
            cm[0, y, :, 3 * dof : 4 * dof] = kh_s[y].T[0:dof].astype(BF16)

    @pl.when(jnp.logical_not(has_s))
    def _():
        for y in range(by):
            cm[0, y, :, 3 * dof : 4 * dof] = zero_block

    def sweep(r, _):
        old = lax.rem(r - 1, 2)

        def sweep_row(k, _):
            x = row_at(k)

            @pl.when(has_w)
            def _():
                face(1, r - 1, x).wait_recv()
                xb[old, x + 1, 0] = h_w[r - 1, x].astype(BF16)

            @pl.when(has_e)
            def _():
                face(0, r - 1, x).wait_recv()
                xb[old, x + 1, by + 1] = h_e[r - 1, x].astype(BF16)

            @pl.when((x == 0) & has_s)
            def _():
                face(3, r - 1, x).wait_recv()
                for y in range(by):
                    xb[old, 0, y + 1] = h_s[r - 1, y].astype(BF16)

            @pl.when((x == bx - 1) & has_n)
            def _():
                face(2, r - 1, x).wait_recv()
                for y in range(by):
                    xb[old, bx + 1, y + 1] = h_n[r - 1, y].astype(BF16)

            for y in range(by):
                near = jnp.concatenate(
                    [xb[old, x + 1, y + 2], xb[old, x + 2, y + 1], xb[old, x + 1, y], xb[old, x, y + 1]],
                    axis=0,
                )
                c = mm(cm[x, y], near)
                t = (loads_ref[x, y].astype(F32) - c[:, 0:lanes]) * rc[x, y]
                tt[r, x, y] = t
                m = mw[x, y]
                u = m * (u_ref[x, y] + RELAXATION * mul3(p3[x, y], t - ku[x, y]))
                finish(r, x, y, u, m * (gh[x, y] - c[:, lanes : 2 * lanes]))
            send_row(r, x)

            @pl.when(r < SWEEPS - 1)
            def _():
                after(x)

            return 0

        return lax.fori_loop(0, bx, sweep_row, 0)

    lax.fori_loop(1, SWEEPS, sweep, 0)

    for x in range(bx):
        for y in range(by):
            total = tt[0, x, y] * x_st[SWEEPS - 1, x, y, :, lanes : 2 * lanes]
            for r in range(1, SWEEPS):
                total = total + tt[r, x, y] * x_st[SWEEPS - 1 - r, x, y, :, lanes : 2 * lanes]
            hi, lo = split(-total)
            b = x * by + y
            acc_hi[:, b * lanes : (b + 1) * lanes] = hi
            acc_lo[:, b * lanes : (b + 1) * lanes] = lo
    sums = mm_nt(oh[...], acc_hi[...]) + mm_nt(oh[...], acc_lo[...])
    sums = jnp.concatenate([sums, jnp.zeros((span, wide - dof), F32)], axis=1)
    placed[...] = sums.reshape(n_sy, groups, wide)

    def grad_copy(k):
        j = lax.rem(sy + k, n_sy)
        return pltpu.make_async_remote_copy(
            src_ref=placed.at[j], dst_ref=back.at[sy], send_sem=sc.at[k], recv_sem=rcs.at[sy],
            device_id=(1 - sec, sx, j), device_id_type=MESH,
        )

    for k in range(n_sy):
        grad_copy(k).start()

    pre_in = pre[...]
    q = jax.nn.sigmoid(pre_in)
    slope = q + pre_in * q * (1.0 - q)

    for j in range(n_sy):
        pltpu.make_async_remote_copy(
            src_ref=placed.at[j], dst_ref=back.at[j], send_sem=sc.at[j], recv_sem=rcs.at[j],
            device_id=(1 - sec, sx, j), device_id_type=MESH,
        ).wait_recv()
    net_grad = jnp.sum(back[...], axis=0)
    g = gate[...]
    out_term = net_grad * (2.0 * g * (1.0 - g))
    spread = jnp.broadcast_to(out_term[:, None, :], (groups, elem, wide)).reshape(n_rows, wide)
    spread = jnp.where(mine, spread, 0.0)
    out_round = spread.astype(BF16)
    turned_out = spread.T.astype(BF16)
    w_out_t = mm(turned_out, hid[...])[0:dof]
    hidden_units = w_out_t.shape[1]
    ex_ref[0:width] = jnp.sum(w_out_t.reshape(elem, width, hidden_units), axis=0)
    in_term = mm(out_round, wt_ref[...]) * slope
    wg_ref[...] = mm(pick_t[...], in_term.astype(BF16))
    tail = jnp.concatenate(
        [
            jnp.sum(in_term, axis=0, keepdims=True),
            jnp.concatenate(
                [jnp.sum(out_term, axis=0, keepdims=True), jnp.zeros((1, hidden_units - wide), F32)], axis=1
            ),
            jnp.zeros((6, hidden_units), F32),
        ],
        axis=0,
    )
    ex_ref[width : width + 8] = tail

    for k in range(n_sy):
        group_copy(k).wait_send()
        grad_copy(k).wait_send()

    @pl.when(has_e)
    def _():
        kw_copy().wait_send()

    @pl.when(has_n)
    def _():
        ks_copy().wait_send()

    for r in range(SWEEPS - 1):
        for x in range(bx):

            @pl.when(has_w)
            def _():
                face(0, r, x).wait_send()

            @pl.when(has_e)
            def _():
                face(1, r, x).wait_send()

        @pl.when(has_s)
        def _():
            face(2, r, 0).wait_send()

        @pl.when(has_n)
        def _():
            face(3, r, 0).wait_send()


def local(
    replay, replay_pick, w_in, b_in, w_out, b_out, block_rows, loads, fixed_mask, elem_map, cotangent
):
    _, bx, by, dof, _ = block_rows.shape
    lanes = loads.shape[-1]
    n_sx, n_sy = lax.axis_size("sx"), lax.axis_size("sy")
    feat, hidden_units = w_in.shape
    ecoef = w_out.shape[1]
    groups = bx * by
    wide = 2 * dof
    picked = replay[:, :, :, 0]
    picked = jnp.where((replay_pick == 1)[..., None, None], replay[:, :, :, 1], picked)
    picked = picked.reshape(-1, feat)
    n_rows = picked.shape[0]
    elem = n_rows // groups
    wt = jnp.concatenate([jnp.tile(w_out.T, (elem, 1)), jnp.zeros((wide - dof, hidden_units), BF16)], axis=0)
    bt = jnp.concatenate([jnp.tile(b_out, elem), jnp.zeros((wide - dof,), F32)])[None]
    mask = fixed_mask.reshape(groups, dof).T.astype(F32)
    vm = lambda: pl.BlockSpec(memory_space=pltpu.VMEM)
    sm = lambda: pl.BlockSpec(memory_space=pltpu.SMEM)
    dma = pltpu.SemaphoreType.DMA
    rounds = SWEEPS - 1
    span = n_sy * groups
    scratch = [
        pltpu.VMEM((n_rows, hidden_units), F32),
        pltpu.VMEM((n_rows, hidden_units), BF16),
        pltpu.VMEM((feat, n_rows), BF16),
        pltpu.VMEM((groups, wide), F32),
        pltpu.VMEM((groups, wide), F32),
        pltpu.VMEM((n_sy, groups, wide), F32),
        pltpu.VMEM((n_sy, groups, wide), F32),
        pltpu.VMEM((n_sy, groups, wide), F32),
        pltpu.VMEM((span, groups * lanes), BF16),
        pltpu.VMEM((bx, dof, 2 * dof), F32),
        pltpu.VMEM((by, dof, 2 * dof), F32),
        pltpu.VMEM((bx, by, dof, 4 * dof), BF16),
        pltpu.VMEM((bx, by, dof, 3 * dof), BF16),
        pltpu.VMEM((bx, by, dof, 3 * dof), BF16),
        pltpu.VMEM((bx, by, dof, 3 * dof), BF16),
        pltpu.VMEM((bx, by, dof, 3 * dof), BF16),
        pltpu.VMEM((bx, by, dof, lanes), F32),
        pltpu.VMEM((bx, by, dof, lanes), F32),
        pltpu.VMEM((bx, by, dof, lanes), F32),
        pltpu.VMEM((SWEEPS, bx, by, dof, 2 * lanes), F32),
        pltpu.VMEM((rounds, bx, dof, 2 * lanes), F32),
        pltpu.VMEM((rounds, bx, dof, 2 * lanes), F32),
        pltpu.VMEM((rounds, by, dof, 2 * lanes), F32),
        pltpu.VMEM((rounds, by, dof, 2 * lanes), F32),
        pltpu.VMEM((2, bx + 2, by + 2, dof, 2 * lanes), BF16),
        pltpu.VMEM((SWEEPS, bx, by, dof, lanes), F32),
        pltpu.VMEM((bx, by, dof, lanes), F32),
        pltpu.VMEM((bx, by, dof, lanes), F32),
        pltpu.VMEM((dof, groups * lanes), BF16),
        pltpu.VMEM((dof, groups * lanes), BF16),
        dma((n_sy,)), dma((n_sy,)), dma((2,)), dma((2,)),
        dma((2, rounds, bx)), dma((2, rounds, bx)), dma((2, rounds)), dma((2, rounds)),
        dma((n_sy,)), dma((n_sy,)),
    ]
    field, wg, ex = pl.pallas_call(
        functools.partial(kernel, n_sx, n_sy),
        out_shape=(
            jax.ShapeDtypeStruct((bx, by, dof, lanes), F32),
            jax.ShapeDtypeStruct((feat, hidden_units), F32),
            jax.ShapeDtypeStruct((ecoef + 8, hidden_units), F32),
        ),
        in_specs=[vm()] * 8 + [sm(), vm()],
        out_specs=(vm(), vm(), vm()),
        scratch_shapes=scratch,
        compiler_params=pltpu.CompilerParams(
            collective_id=0, has_side_effects=True, vmem_limit_bytes=48 * 1024 * 1024
        ),
    )(picked, w_in, b_in[None], wt, bt, block_rows[0], loads[0], mask, elem_map[0], cotangent[0])
    wg, ex = lax.psum((wg, ex), ("sec", "sx", "sy"))
    w_out_grad = ex[0:ecoef].T
    b_in_grad = ex[ecoef]
    b_out_grad = jnp.sum(ex[ecoef + 1, 0:dof].reshape(elem, ecoef), axis=0)
    return (field[None], wg, b_in_grad, w_out_grad, b_out_grad)


def solution(mesh):
    placed = (
        P("sec", "sx", "sy", None, None, None),
        P("sec", "sx", "sy"),
        P(),
        P(),
        P(),
        P(),
        P("sec", "sx", "sy", None, None),
        P("sec", "sx", "sy", None, None),
        P("sec", "sx", "sy", None),
        P("sec", "sx", "sy"),
        P("sec", "sx", "sy", None, None),
    )
    return jax.shard_map(
        local,
        mesh=mesh,
        in_specs=placed,
        out_specs=(P("sec", "sx", "sy", None, None), P(), P(), P(), P()),
        check_vma=False,
    )
```

profile of v0, /device:TPU:1, one launch (start us, length us, event | category | flops | bytes accessed | tf_op | source)
XLA Modules:
  0.0 190.4 jit_solution(6057939155339393390)
XLA Ops:
  7.2 0.0 copy-start
  7.2 0.0 copy-start.9
  7.2 0.0 all-reduce.4.cloned.1.call-start
  7.2 0.0 copy-start.4
  7.2 0.9 fusion
  8.2 0.0 copy-done.9
  8.2 0.1 broadcast_in_dim.27
  8.3 0.0 copy-start.8
  8.3 0.0 copy-start.10
  8.3 0.1 broadcast_in_dim.28
  8.4 0.0 copy-done
  8.4 0.0 copy-start.2
  8.4 0.0 copy-start.3
  8.4 0.6 copy-done.8
  9.0 0.1 copy.17
  9.1 0.0 copy-done.10
  9.1 0.1 tile.21
  9.2 0.1 bitcast_select_fusion.picked_ref
  9.3 0.0 copy-start.6
  9.3 0.0 copy-start.5
  9.3 0.0 copy-done.4
  9.3 0.0 copy-done.2
  9.3 0.1 copy-done.3
  9.4 0.6 copy-done.6
  10.0 0.0 copy-done.5
  10.0 0.0 copy-start.1
  10.0 1.2 copy-done.1
  11.2 45.9 %shard_map.146 = (f32[4,4,64,128]{3,2,1,0:T(8,128)S(1)}, f32[256,512]{1,0:T(8,128)}, f32[16,512]{1,0:T(8,128)S(1)}) custom-call(bf16[128,256]{1,0:T(8,128)(2,1)S(1)} %bitcast_select_fusion.picked_ref, bf16[256,512]{1,0:T(8,128)(2,1)S(1)} %copy-done.2, f32[1,512]{1,0:T(1,128)S(1)} %bitcast.28, bf16[128,512]{1,0:T(8,128)(2,1)S(1)} %concatenate.6.wt_ref, ...), custom_call_target="tpu_custom_call" | custom-call | tf_op jit(solution)/shard_map/pallas_call | solution.py:452
  57.2 0.0 all-reduce.4.cloned.1.call-update
  57.2 38.1 %psum.15 = f32[16,512]{1,0:T(8,128)S(1)} all-reduce(f32[16,512]{1,0:T(8,128)S(1)} %get-tuple-element.10), channel_id=1, replica_groups=mesh['sec'=2,'sx'=2,'sy'=8] {'sec','sx','sy'}, use_global_device_ids=true, to_apply=%region_1.2 | all-reduce | flops 8192 | bytes 65536 | tf_op jit(solution)/shard_map/psum | solution.py:466
  95.3 0.6 slice.20
  95.9 0.1 reshape_squeeze.3
  96.0 0.5 reduce_sum.9
  96.5 0.6 slice_bitcast_fusion
  97.1 84.4 %all-reduce.4.cloned.1.call-done = f32[256,512]{1,0:T(8,128)} async-done(((f32[256,512]{1,0:T(8,128)}), f32[256,512]{1,0:T(8,128)}) %all-reduce.4.cloned.1.call-update) | async-done | bytes 524304 | tf_op jit(solution)/shard_map/psum | solution.py:466
  181.6 0.0 copy-start.7
  181.6 0.8 copy.21
  182.4 0.4 copy-done.7
  182.8 0.8 copy.22
  (7 shorter events, 0.1 us)
Async XLA Ops:
  7.2 1.2 copy-start
  7.2 1.0 copy-start.9
  7.2 174.4 %all-reduce.4.cloned.1.call-start = ((), (), s32[]{:S(2)}) async-start(), calls=%async_computation | async-start | bytes 1048576 | tf_op jit(solution)/shard_map/psum | solution.py:466
  7.2 2.1 %copy-start.4 = (bf16[1,4,4,64,128]{4,3,2,1,0:T(8,128)(2,1)S(1)}, bf16[1,4,4,64,128]{4,3,2,1,0:T(8,128)(2,1)}, u32[]{:S(2)}) copy-start(bf16[1,4,4,64,128]{4,3,2,1,0:T(8,128)(2,1)} %param.21) | copy-start | bytes 786436
  8.3 0.7 copy-start.8
  8.3 0.8 copy-start.10
  8.4 1.0 copy-start.2
  8.4 1.0 copy-start.3
  9.3 0.7 copy-start.6
  9.3 0.7 copy-start.5
  10.0 1.2 copy-start.1
  181.6 1.2 copy-start.7
Sparse Core Ops, SparseCore 0:
  57.3 124.2 all-reduce.3
where the time goes:
time: 192 us; the launch traced here: 190 us
  waiting for transfers between devices  84.4 us (44%)
  Pallas kernels  45.9 us (24%)
  blocking collectives  38.1 us (20%)
  between operations  14.2 us (7%)
  local copies, waits for them, and re-layouts  7.1 us (4%)
    psum x1, waiting for transfers between devices, local(): wg, ex = lax.psum((wg, ex), ('sec', 'sx', 'sy'))  84.4 us
    pallas_call x1, Pallas kernels, local(): pl.pallas_call(functools.partial(kernel, n_sx, n_sy), out_shape=(jax.Shap...  45.9 us
    psum x1, blocking collectives, local(): wg, ex = lax.psum((wg, ex), ('sec', 'sx', 'sy'))  38.1 us
    unnamed x24, local copies, waits for them, and re-layouts  4.53 us
  transfers between devices with their start and end apart: 1, of which 1 were waited for; matrix products, arithmetic and copies ran while one was open for 1% of the time, Pallas kernels for 0%

commit v1 on v0

--- a/solution.py
+++ b/solution.py
@@ -43,10 +43,11 @@
 
 def kernel(
     n_sx, n_sy, picked_ref, w_in_ref, b_in_ref, wt_ref, b_out_ref, rows_ref, loads_ref, mask_ref, map_ref,
-    cot_ref, u_ref, wg_ref, ex_ref,
+    cot_ref, u_ref, wg_ref, bi_ref, wo_ref, bo_ref,
     pre, hid, pick_t, gate, own, gath, placed, back, oh, kh_w, kh_s, cm, kd3, kdt3, p3, pt3, mw, cw, rc,
     x_st, h_w, h_e, h_s, h_n, xb, tt, ku, gh, acc_hi, acc_lo,
-    sg, rg, sk, rk, s_we, r_we, s_ns, r_ns, sc, rcs,
+    red, half, got_core, got_plane, got_z, summed,
+    sg, rg, sk, rk, s_we, r_we, s_ns, r_ns, sc, rcs, s_core, r_core, s_plane, r_plane, s_z, r_z,
 ):
     bx, by, dof = rows_ref.shape[0], rows_ref.shape[1], rows_ref.shape[2]
     groups = bx * by
@@ -56,7 +57,20 @@
     west, east = (sec, sx, sy - 1), (sec, sx, sy + 1)
     south, north = (sec, sx - 1, sy), (sec, sx + 1, sy)
 
+    n_plane, n_z = 2 * n_sx, n_sy // 2
+    core, my_z, my_plane = lax.rem(sy, 2), sy // 2, sec * n_sx + sx
+    mate = (sec, sx, sy + 1 - 2 * core)
+    plane_dev = lambda i: (i // n_sx, lax.rem(i, n_sx), sy)
+    z_dev = lambda i: (sec, sx, 2 * i + core)
+
     barrier = pltpu.get_barrier_semaphore()
+    pl.semaphore_signal(barrier, inc=1, device_id=mate, device_id_type=MESH)
+    for k in range(1, n_plane):
+        pl.semaphore_signal(
+            barrier, inc=1, device_id=plane_dev(lax.rem(my_plane + k, n_plane)), device_id_type=MESH
+        )
+    for k in range(1, n_z):
+        pl.semaphore_signal(barrier, inc=1, device_id=z_dev(lax.rem(my_z + k, n_z)), device_id_type=MESH)
     for k in range(n_sy):
         pl.semaphore_signal(
             barrier, inc=1, device_id=(1 - sec, sx, lax.rem(sy + k, n_sy)), device_id_type=MESH
@@ -84,7 +98,7 @@
     own[...] = 0.5 + 2.0 * gate_rows
 
     one = lambda has: jnp.where(has, 1, 0)
-    pl.semaphore_wait(barrier, n_sy + one(has_w) + one(has_e) + one(has_s) + one(has_n))
+    pl.semaphore_wait(barrier, n_sy + n_plane + n_z - 1 + one(has_w) + one(has_e) + one(has_s) + one(has_n))
 
     def group_copy(k):
         j = lax.rem(sy + k, n_sy)
@@ -344,11 +358,11 @@
     turned_out = spread.T.astype(BF16)
     w_out_t = mm(turned_out, hid[...])[0:dof]
     hidden_units = w_out_t.shape[1]
-    ex_ref[0:width] = jnp.sum(w_out_t.reshape(elem, width, hidden_units), axis=0)
     in_term = mm(out_round, wt_ref[...]) * slope
-    wg_ref[...] = mm(pick_t[...], in_term.astype(BF16))
-    tail = jnp.concatenate(
+    w_in_grad = mm(pick_t[...], in_term.astype(BF16))
+    extra = jnp.concatenate(
         [
+            jnp.sum(w_out_t.reshape(elem, width, hidden_units), axis=0),
             jnp.sum(in_term, axis=0, keepdims=True),
             jnp.concatenate(
                 [jnp.sum(out_term, axis=0, keepdims=True), jnp.zeros((1, hidden_units - wide), F32)], axis=1
@@ -357,8 +371,103 @@
         ],
         axis=0,
     )
-    ex_ref[width : width + 8] = tail
-
+
+    feat = w_in_grad.shape[0]
+    strips, deep, more = hidden_units // 128, feat // 8, extra.shape[0] // 8
+    tiles = red.shape[0]
+    n_half, per = tiles // 2, got_z.shape[1]
+    used = strips * (deep + more)
+    for c in range(strips):
+        red[c * deep : (c + 1) * deep] = w_in_grad[:, c * 128 : (c + 1) * 128].reshape(deep, 8, 128)
+        at = strips * deep + c * more
+        red[at : at + more] = extra[:, c * 128 : (c + 1) * 128].reshape(more, 8, 128)
+    if used < tiles:
+        red[used:tiles] = jnp.zeros((tiles - used, 8, 128), F32)
+
+    def core_copy(step, src, dst):
+        return pltpu.make_async_remote_copy(
+            src_ref=src, dst_ref=dst, send_sem=s_core.at[step], recv_sem=r_core.at[step],
+            device_id=mate, device_id_type=MESH,
+        )
+
+    give = core_copy(0, red.at[pl.ds((1 - core) * n_half, n_half)], got_core)
+    give.start()
+    give.wait_recv()
+    half[...] = red[pl.ds(core * n_half, n_half)] + got_core[...]
+
+    def plane_copy(step, k, src, dst, slot):
+        return pltpu.make_async_remote_copy(
+            src_ref=src, dst_ref=dst, send_sem=s_plane.at[step, k], recv_sem=r_plane.at[step, slot],
+            device_id=plane_dev(lax.rem(my_plane + k, n_plane)), device_id_type=MESH,
+        )
+
+    def plane_give(k):
+        to = lax.rem(my_plane + k, n_plane)
+        return plane_copy(0, k, half.at[pl.ds(to * per, per)], got_plane.at[my_plane], my_plane)
+
+    def plane_got(k):
+        source = lax.rem(my_plane + k, n_plane)
+        return plane_copy(0, k, half.at[pl.ds(0, per)], got_plane.at[source], source)
+
+    for k in range(1, n_plane):
+        plane_give(k).start()
+    part = half[pl.ds(my_plane * per, per)]
+    for k in range(1, n_plane):
+        plane_got(k).wait_recv()
+        part = part + got_plane[lax.rem(my_plane + k, n_plane)]
+    got_z[my_z] = part
+
+    def z_copy(k, slot):
+        return pltpu.make_async_remote_copy(
+            src_ref=got_z.at[my_z], dst_ref=got_z.at[slot], send_sem=s_z.at[k], recv_sem=r_z.at[slot],
+            device_id=z_dev(lax.rem(my_z + k, n_z)), device_id_type=MESH,
+        )
+
+    for k in range(1, n_z):
+        z_copy(k, my_z).start()
+    for k in range(1, n_z):
+        z_copy(k, lax.rem(my_z + k, n_z)).wait_recv()
+    base = core * n_half
+    mine_at = pl.ds(base + my_plane * per, per)
+    summed[mine_at] = jnp.sum(got_z[...], axis=0)
+
+    def plane_spread(k):
+        return plane_copy(1, k, summed.at[mine_at], summed.at[mine_at], my_plane)
+
+    def plane_fill(k):
+        source = lax.rem(my_plane + k, n_plane)
+        there = summed.at[pl.ds(base + source * per, per)]
+        return plane_copy(1, k, there, there, source)
+
+    for k in range(1, n_plane):
+        plane_spread(k).start()
+    for k in range(1, n_plane):
+        plane_fill(k).wait_recv()
+    spread_half = core_copy(1, summed.at[pl.ds(base, n_half)], summed.at[pl.ds(base, n_half)])
+    spread_half.start()
+    other = summed.at[pl.ds((1 - core) * n_half, n_half)]
+    core_copy(1, other, other).wait_recv()
+
+    sums = []
+    for c in range(strips):
+        wg_ref[:, c * 128 : (c + 1) * 128] = summed[c * deep : (c + 1) * deep].reshape(feat, 128)
+        at = strips * deep + c * more
+        piece = summed[at : at + more].reshape(8 * more, 128)
+        wo_ref[c * 128 : (c + 1) * 128, :] = piece.T[:, 0:width]
+        bi_ref[:, c * 128 : (c + 1) * 128] = piece[width : width + 1]
+        if c == 0:
+            folded = piece[width + 1 : width + 2, 0:width]
+            for e in range(1, elem):
+                folded = folded + piece[width + 1 : width + 2, e * width : (e + 1) * width]
+            bo_ref[...] = folded
+
+    give.wait_send()
+    spread_half.wait_send()
+    for k in range(1, n_plane):
+        plane_give(k).wait_send()
+        plane_spread(k).wait_send()
+    for k in range(1, n_z):
+        z_copy(k, my_z).wait_send()
     for k in range(n_sy):
         group_copy(k).wait_send()
         grad_copy(k).wait_send()
@@ -414,6 +523,10 @@
     dma = pltpu.SemaphoreType.DMA
     rounds = SWEEPS - 1
     span = n_sy * groups
+    n_plane, n_z = 2 * n_sx, n_sy // 2
+    needed = (feat + ecoef + 8) * hidden_units // 1024
+    per = -(-needed // (2 * n_plane))
+    tiles = 2 * n_plane * per
     scratch = [
         pltpu.VMEM((n_rows, hidden_units), F32),
         pltpu.VMEM((n_rows, hidden_units), BF16),
@@ -445,29 +558,34 @@
         pltpu.VMEM((bx, by, dof, lanes), F32),
         pltpu.VMEM((dof, groups * lanes), BF16),
         pltpu.VMEM((dof, groups * lanes), BF16),
+        pltpu.VMEM((tiles, 8, 128), F32),
+        pltpu.VMEM((tiles // 2, 8, 128), F32),
+        pltpu.VMEM((tiles // 2, 8, 128), F32),
+        pltpu.VMEM((n_plane, per, 8, 128), F32),
+        pltpu.VMEM((n_z, per, 8, 128), F32),
+        pltpu.VMEM((tiles, 8, 128), F32),
         dma((n_sy,)), dma((n_sy,)), dma((2,)), dma((2,)),
         dma((2, rounds, bx)), dma((2, rounds, bx)), dma((2, rounds)), dma((2, rounds)),
         dma((n_sy,)), dma((n_sy,)),
+        dma((2,)), dma((2,)), dma((2, n_plane)), dma((2, n_plane)), dma((n_z,)), dma((n_z,)),
     ]
-    field, wg, ex = pl.pallas_call(
+    field, w_in_grad, b_in_grad, w_out_grad, b_out_grad = pl.pallas_call(
         functools.partial(kernel, n_sx, n_sy),
         out_shape=(
             jax.ShapeDtypeStruct((bx, by, dof, lanes), F32),
             jax.ShapeDtypeStruct((feat, hidden_units), F32),
-            jax.ShapeDtypeStruct((ecoef + 8, hidden_units), F32),
+            jax.ShapeDtypeStruct((1, hidden_units), F32),
+            jax.ShapeDtypeStruct((hidden_units, ecoef), F32),
+            jax.ShapeDtypeStruct((1, ecoef), F32),
         ),
         in_specs=[vm()] * 8 + [sm(), vm()],
-        out_specs=(vm(), vm(), vm()),
+        out_specs=(vm(), vm(), vm(), vm(), vm()),
         scratch_shapes=scratch,
         compiler_params=pltpu.CompilerParams(
             collective_id=0, has_side_effects=True, vmem_limit_bytes=48 * 1024 * 1024
         ),
     )(picked, w_in, b_in[None], wt, bt, block_rows[0], loads[0], mask, elem_map[0], cotangent[0])
-    wg, ex = lax.psum((wg, ex), ("sec", "sx", "sy"))
-    w_out_grad = ex[0:ecoef].T
-    b_in_grad = ex[ecoef]
-    b_out_grad = jnp.sum(ex[ecoef + 1, 0:dof].reshape(elem, ecoef), axis=0)
-    return (field[None], wg, b_in_grad, w_out_grad, b_out_grad)
+    return (field[None], w_in_grad, b_in_grad[0], w_out_grad, b_out_grad[0])
 
 
 def solution(mesh):

time: 192 us -> 74.1 us (0.39)
  waiting for transfers between devices: 84.4 us -> 0 us
  blocking collectives: 38.1 us -> 0 us
  Pallas kernels: 45.9 us -> 64.6 us
  between operations: 14.2 us -> 0.76 us
    psum x1 -> x0, waiting for transfers between devices: 84.4 us -> none  [local(): wg, ex = lax.psum((wg, ex), ('sec', 'sx', 'sy'))]
    psum x1 -> x0, blocking collectives: 38.1 us -> none  [local(): wg, ex = lax.psum((wg, ex), ('sec', 'sx', 'sy'))]
    pallas_call x1, Pallas kernels: 45.9 us -> 64.6 us  [local(): pl.pallas_call(functools.partial(kernel, n_sx, n_sy), out_shape=(jax.Shap...]
    unnamed x24 -> x25, local copies, waits for them, and re-layouts: 4.53 us -> 7.06 us
  transfers between devices with their start and end apart: 1 -> 0, of which waited for: 1 -> 0; matrix products, arithmetic and copies ran while one was open for 1% -> 0% of each run, Pallas kernels for 0% -> 0%
where the time goes in v1:
time: 74.1 us; the launch traced here: 73.8 us
  Pallas kernels  64.6 us (87%)
  local copies, waits for them, and re-layouts  8.35 us (11%)
  between operations  0.76 us (1%)
    pallas_call x1, Pallas kernels, local(): pl.pallas_call(functools.partial(kernel, n_sx, n_sy), out_shape=(jax.Shap...  64.6 us
    unnamed x25, local copies, waits for them, and re-layouts  7.06 us

profile of v1, /device:TPU:1, one launch (start us, length us, event | category | flops | bytes accessed | tf_op | source)
XLA Modules:
  0.0 73.8 jit_solution(14547339880913163203)
XLA Ops:
  0.6 0.0 copy-start
  0.6 0.7 copy-done
  1.3 0.0 copy-start.8
  1.3 0.7 copy-done.8
  2.0 0.0 copy-start.9
  2.0 0.0 copy-start.7
  2.0 0.1 broadcast_in_dim.27
  2.1 0.1 broadcast_in_dim.28
  2.2 0.5 copy-done.9
  2.7 0.1 tile.21
  2.8 0.0 copy-done.7
  2.8 0.0 copy-start.4
  2.8 0.1 copy.18
  2.9 0.0 copy-start.3
  2.9 0.0 copy-start.2
  2.9 0.9 %fusion = (bf16[1,4,4,1,8,256]{5,4,3,2,1,0:T(8,128)(2,1)S(1)}, bf16[1,4,4,1,8,256]{5,4,3,2,1,0:T(8,128)(2,1)S(1)}) fusion(bf16[1,4,4,2,8,256]{5,4,3,2,1,0:T(8,128)(2,1)} %param.11), kind=kLoop, calls=%fused_computation.4 | loop fusion | bytes 262144 | tf_op jit(solution)/shard_map/slice | solution.py:514
  3.9 0.0 copy-start.5
  3.9 0.0 copy-start.6
  3.9 0.1 bitcast_select_fusion.picked_ref
  4.0 0.0 copy-done.4
  4.0 0.0 copy-done.3
  4.0 0.0 copy-done.2
  4.0 0.6 copy-done.5
  4.6 0.0 copy-done.6
  4.6 0.0 copy-start.1
  4.6 1.2 %copy-done.1 = f32[1,4,4,64,256]{4,3,2,1,0:T(8,128)S(1)} copy-done((f32[1,4,4,64,256]{4,3,2,1,0:T(8,128)S(1)}, f32[1,4,4,64,256]{4,3,2,1,0:T(8,128)}, u32[]{:S(2)}) %copy-start.1) | copy-done | bytes 1048600
  5.8 64.6 %shard_map.146 = (f32[4,4,64,128]{3,2,1,0:T(8,128)S(1)}, f32[256,512]{1,0:T(8,128)S(1)}, f32[1,512]{1,0:T(1,128)S(1)}, f32[512,8]{1,0:T(8,128)S(1)}, f32[1,8]{1,0:T(1,128)S(1)}) custom-call(bf16[128,256]{1,0:T(8,128)(2,1)S(1)} %bitcast_select_fusion.picked_ref, bf16[256,512]{1,0:T(8,128)(2,1)S(1)} %copy-done.2, f32[1,512]{1,0:T(1,128)S(1)} %bitcast.27, ...), custom_call_target="tpu_custom_call" | custom-call | tf_op jit(solution)/shard_map/pallas_call | solution.py:572
  70.4 0.7 copy.19
  71.1 0.8 %copy.24 = f32[1,4,4,64,128]{4,3,2,1,0:T(8,128)} copy(f32[1,4,4,64,128]{4,3,2,1,0:T(8,128)S(1)} %bitcast.23) | data formatting | bytes 1048576
  71.9 0.8 %copy.25 = f32[256,512]{1,0:T(8,128)} copy(f32[256,512]{1,0:T(8,128)S(1)} %get-tuple-element.33) | data formatting | bytes 1048576
  72.7 0.6 copy.26
  73.3 0.5 copy.27
  (6 shorter events, 0.0 us)
Async XLA Ops:
  0.6 0.7 copy-start
  1.3 0.7 copy-start.8
  2.0 0.7 copy-start.9
  2.0 0.7 %copy-start.7 = (s32[1,4,4,64]{3,2,1,0:T(4,128)S(1)}, s32[1,4,4,64]{3,2,1,0:T(4,128)}, u32[]{:S(2)}) copy-start(s32[1,4,4,64]{3,2,1,0:T(4,128)} %param.19) | copy-start | bytes 12292
  2.8 1.2 %copy-start.4 = (bf16[1,4,4,64,128]{4,3,2,1,0:T(8,128)(2,1)S(1)}, bf16[1,4,4,64,128]{4,3,2,1,0:T(8,128)(2,1)}, u32[]{:S(2)}) copy-start(bf16[1,4,4,64,128]{4,3,2,1,0:T(8,128)(2,1)} %param.21) | copy-start | bytes 786436
  2.9 1.1 %copy-start.3 = (bf16[1,4,4,64,128]{4,3,2,1,0:T(8,128)(2,1)S(1)}, bf16[1,4,4,64,128]{4,3,2,1,0:T(8,128)(2,1)}, u32[]{:S(2)}) copy-start(bf16[1,4,4,64,128]{4,3,2,1,0:T(8,128)(2,1)} %param.18) | copy-start | bytes 786436
  2.9 1.1 %copy-start.2 = (bf16[256,512]{1,0:T(8,128)(2,1)S(1)}, bf16[256,512]{1,0:T(8,128)(2,1)}, u32[]{:S(2)}) copy-start(bf16[256,512]{1,0:T(8,128)(2,1)} %w_in_ref.1) | copy-start | bytes 786436
  3.9 0.7 copy-start.5
  3.9 0.7 copy-start.6
  4.6 1.2 %copy-start.1 = (f32[1,4,4,64,256]{4,3,2,1,0:T(8,128)S(1)}, f32[1,4,4,64,256]{4,3,2,1,0:T(8,128)}, u32[]{:S(2)}) copy-start(f32[1,4,4,64,256]{4,3,2,1,0:T(8,128)} %param.17) | copy-start | bytes 3145732

commit v2 on v1

--- a/solution.py
+++ b/solution.py
@@ -42,16 +42,22 @@
 
 
 def kernel(
-    n_sx, n_sy, picked_ref, w_in_ref, b_in_ref, wt_ref, b_out_ref, rows_ref, loads_ref, mask_ref, map_ref,
-    cot_ref, u_ref, wg_ref, bi_ref, wo_ref, bo_ref,
+    n_sx, n_sy, picked_ref, w_in_ref, b_in_ref, wt_ref, b_out_ref, rows_in, loads_in, mask_ref, map_ref,
+    cot_in, u_ref, wg_ref, bi_ref, wo_ref, bo_ref,
     pre, hid, pick_t, gate, own, gath, placed, back, oh, kh_w, kh_s, cm, kd3, kdt3, p3, pt3, mw, cw, rc,
     x_st, h_w, h_e, h_s, h_n, xb, tt, ku, gh, acc_hi, acc_lo,
-    red, half, got_core, got_plane, got_z, summed,
+    red, half, got_core, got_plane, got_z, summed, rows_ref, loads_ref, cot_ref, s_in,
     sg, rg, sk, rk, s_we, r_we, s_ns, r_ns, sc, rcs, s_core, r_core, s_plane, r_plane, s_z, r_z,
 ):
     bx, by, dof = rows_ref.shape[0], rows_ref.shape[1], rows_ref.shape[2]
     groups = bx * by
     lanes = loads_ref.shape[3]
+    fetches = [
+        pltpu.make_async_copy(src, dst, s_in.at[i])
+        for i, (src, dst) in enumerate(((rows_in, rows_ref), (loads_in, loads_ref), (cot_in, cot_ref)))
+    ]
+    for fetch in fetches:
+        fetch.start()
     sec, sx, sy = lax.axis_index("sec"), lax.axis_index("sx"), lax.axis_index("sy")
     has_w, has_e, has_s, has_n = sy > 0, sy < n_sy - 1, sx > 0, sx < n_sx - 1
     west, east = (sec, sx, sy - 1), (sec, sx, sy + 1)
@@ -109,6 +115,8 @@
 
     for k in range(n_sy):
         group_copy(k).start()
+    for fetch in fetches:
+        fetch.wait()
 
     def kw_copy():
         return pltpu.make_async_remote_copy(
@@ -210,39 +218,50 @@
         def _():
             face(1, r, x).start()
 
-    def row_at(k):
-        return jnp.where(sx == 0, k, bx - 1 - k)
-
-    def finish(r, x, y, u, h):
-        m = mw[x, y]
-        p = RELAXATION * mul3(pt3[x, y], h)
-        w = p * rc[x, y]
-        x_st[r, x, y, :, 0:lanes] = u
-        x_st[r, x, y, :, lanes : 2 * lanes] = w
+    step = 2 if bx % 2 == 0 else 1
+
+    def rows_at(k):
+        first = k * step
+        return [jnp.where(sx == 0, first + i, bx - 1 - first - i) for i in range(step)]
+
+    def cells(rows):
+        return [(x, y) for x in rows for y in range(by)]
+
+    def finish(r, at, us, hs):
+        ps = [RELAXATION * mul3(pt3[c], h) for c, h in zip(at, hs)]
+        ws = [p * rc[c] for c, p in zip(at, ps)]
         slot = lax.rem(r, 2)
-        xb[slot, x + 1, y + 1, :, 0:lanes] = u.astype(BF16)
-        xb[slot, x + 1, y + 1, :, lanes : 2 * lanes] = w.astype(BF16)
-        u_ref[x, y] = u
-        gh[x, y] = h
-        cw[x, y] = p
-
-    def after(x):
-        for y in range(by):
-            gh[x, y] = gh[x, y] - mul3(kdt3[x, y], cw[x, y])
-            ku[x, y] = mul3(kd3[x, y], u_ref[x, y])
-
-    def first_row(k, _):
-        x = row_at(k)
-        for y in range(by):
-            t = loads_ref[x, y].astype(F32) * rc[x, y]
-            tt[0, x, y] = t
-            u = mw[x, y] * (RELAXATION * mul3(p3[x, y], t))
-            finish(0, x, y, u, mw[x, y] * cot_ref[x, y].astype(F32))
-        send_row(0, x)
-        after(x)
+        for (x, y), u, h, p, w in zip(at, us, hs, ps, ws):
+            x_st[r, x, y, :, 0:lanes] = u
+            x_st[r, x, y, :, lanes : 2 * lanes] = w
+            xb[slot, x + 1, y + 1, :, 0:lanes] = u.astype(BF16)
+            xb[slot, x + 1, y + 1, :, lanes : 2 * lanes] = w.astype(BF16)
+            u_ref[x, y] = u
+            gh[x, y] = h
+            cw[x, y] = p
+
+    def after(at):
+        gs = [gh[c] - mul3(kdt3[c], cw[c]) for c in at]
+        ks = [mul3(kd3[c], u_ref[c]) for c in at]
+        for c, g, k in zip(at, gs, ks):
+            gh[c] = g
+            ku[c] = k
+
+    def first_rows(k, _):
+        rows = rows_at(k)
+        at = cells(rows)
+        ts = [loads_ref[c].astype(F32) * rc[c] for c in at]
+        us = [mw[c] * (RELAXATION * mul3(p3[c], t)) for c, t in zip(at, ts)]
+        hs = [mw[c] * cot_ref[c].astype(F32) for c in at]
+        finish(0, at, us, hs)
+        for c, t in zip(at, ts):
+            tt[(0, *c)] = t
+        for x in rows:
+            send_row(0, x)
+        after(at)
         return 0
 
-    lax.fori_loop(0, bx, first_row, 0)
+    lax.fori_loop(0, bx // step, first_rows, 0)
 
     @pl.when(has_w)
     def _():
@@ -269,51 +288,55 @@
     def sweep(r, _):
         old = lax.rem(r - 1, 2)
 
-        def sweep_row(k, _):
-            x = row_at(k)
-
-            @pl.when(has_w)
-            def _():
-                face(1, r - 1, x).wait_recv()
-                xb[old, x + 1, 0] = h_w[r - 1, x].astype(BF16)
-
-            @pl.when(has_e)
-            def _():
-                face(0, r - 1, x).wait_recv()
-                xb[old, x + 1, by + 1] = h_e[r - 1, x].astype(BF16)
-
-            @pl.when((x == 0) & has_s)
-            def _():
-                face(3, r - 1, x).wait_recv()
-                for y in range(by):
-                    xb[old, 0, y + 1] = h_s[r - 1, y].astype(BF16)
-
-            @pl.when((x == bx - 1) & has_n)
-            def _():
-                face(2, r - 1, x).wait_recv()
-                for y in range(by):
-                    xb[old, bx + 1, y + 1] = h_n[r - 1, y].astype(BF16)
-
-            for y in range(by):
+        def sweep_rows(k, _):
+            rows = rows_at(k)
+            for x in rows:
+                @pl.when(has_w)
+                def _():
+                    face(1, r - 1, x).wait_recv()
+                    xb[old, x + 1, 0] = h_w[r - 1, x].astype(BF16)
+
+                @pl.when(has_e)
+                def _():
+                    face(0, r - 1, x).wait_recv()
+                    xb[old, x + 1, by + 1] = h_e[r - 1, x].astype(BF16)
+
+                @pl.when((x == 0) & has_s)
+                def _():
+                    face(3, r - 1, x).wait_recv()
+                    for y in range(by):
+                        xb[old, 0, y + 1] = h_s[r - 1, y].astype(BF16)
+
+                @pl.when((x == bx - 1) & has_n)
+                def _():
+                    face(2, r - 1, x).wait_recv()
+                    for y in range(by):
+                        xb[old, bx + 1, y + 1] = h_n[r - 1, y].astype(BF16)
+
+            at = cells(rows)
+            cs = []
+            for x, y in at:
                 near = jnp.concatenate(
                     [xb[old, x + 1, y + 2], xb[old, x + 2, y + 1], xb[old, x + 1, y], xb[old, x, y + 1]],
                     axis=0,
                 )
-                c = mm(cm[x, y], near)
-                t = (loads_ref[x, y].astype(F32) - c[:, 0:lanes]) * rc[x, y]
-                tt[r, x, y] = t
-                m = mw[x, y]
-                u = m * (u_ref[x, y] + RELAXATION * mul3(p3[x, y], t - ku[x, y]))
-                finish(r, x, y, u, m * (gh[x, y] - c[:, lanes : 2 * lanes]))
-            send_row(r, x)
+                cs.append(mm(cm[x, y], near))
+            ts = [(loads_ref[a].astype(F32) - c[:, 0:lanes]) * rc[a] for a, c in zip(at, cs)]
+            hs = [mw[a] * (gh[a] - c[:, lanes : 2 * lanes]) for a, c in zip(at, cs)]
+            us = [mw[a] * (u_ref[a] + RELAXATION * mul3(p3[a], t - ku[a])) for a, t in zip(at, ts)]
+            finish(r, at, us, hs)
+            for c, t in zip(at, ts):
+                tt[(r, *c)] = t
+            for x in rows:
+                send_row(r, x)
 
             @pl.when(r < SWEEPS - 1)
             def _():
-                after(x)
+                after(at)
 
             return 0
 
-        return lax.fori_loop(0, bx, sweep_row, 0)
+        return lax.fori_loop(0, bx // step, sweep_rows, 0)
 
     lax.fori_loop(1, SWEEPS, sweep, 0)
 
@@ -453,7 +476,7 @@
         wg_ref[:, c * 128 : (c + 1) * 128] = summed[c * deep : (c + 1) * deep].reshape(feat, 128)
         at = strips * deep + c * more
         piece = summed[at : at + more].reshape(8 * more, 128)
-        wo_ref[c * 128 : (c + 1) * 128, :] = piece.T[:, 0:width]
+        wo_ref[:, c * 128 : (c + 1) * 128] = piece[0:width]
         bi_ref[:, c * 128 : (c + 1) * 128] = piece[width : width + 1]
         if c == 0:
             folded = piece[width + 1 : width + 2, 0:width]
@@ -498,6 +521,15 @@
         @pl.when(has_n)
         def _():
             face(3, r, 0).wait_send()
+
+
+def write_out(*refs):
+    sem = refs[-1]
+    copies = [pltpu.make_async_copy(refs[i], refs[i + 5], sem.at[i]) for i in range(5)]
+    for c in copies:
+        c.start()
+    for c in copies:
+        c.wait()
 
 
 def local(
@@ -519,6 +551,7 @@
     bt = jnp.concatenate([jnp.tile(b_out, elem), jnp.zeros((wide - dof,), F32)])[None]
     mask = fixed_mask.reshape(groups, dof).T.astype(F32)
     vm = lambda: pl.BlockSpec(memory_space=pltpu.VMEM)
+    hbm = lambda: pl.BlockSpec(memory_space=pl.ANY)
     sm = lambda: pl.BlockSpec(memory_space=pltpu.SMEM)
     dma = pltpu.SemaphoreType.DMA
     rounds = SWEEPS - 1
@@ -564,28 +597,39 @@
         pltpu.VMEM((n_plane, per, 8, 128), F32),
         pltpu.VMEM((n_z, per, 8, 128), F32),
         pltpu.VMEM((tiles, 8, 128), F32),
+        pltpu.VMEM(block_rows.shape[1:], F32),
+        pltpu.VMEM(loads.shape[1:], BF16),
+        pltpu.VMEM(cotangent.shape[1:], BF16),
+        dma((3,)),
         dma((n_sy,)), dma((n_sy,)), dma((2,)), dma((2,)),
         dma((2, rounds, bx)), dma((2, rounds, bx)), dma((2, rounds)), dma((2, rounds)),
         dma((n_sy,)), dma((n_sy,)),
         dma((2,)), dma((2,)), dma((2, n_plane)), dma((2, n_plane)), dma((n_z,)), dma((n_z,)),
     ]
-    field, w_in_grad, b_in_grad, w_out_grad, b_out_grad = pl.pallas_call(
+    results = pl.pallas_call(
         functools.partial(kernel, n_sx, n_sy),
         out_shape=(
             jax.ShapeDtypeStruct((bx, by, dof, lanes), F32),
             jax.ShapeDtypeStruct((feat, hidden_units), F32),
             jax.ShapeDtypeStruct((1, hidden_units), F32),
-            jax.ShapeDtypeStruct((hidden_units, ecoef), F32),
+            jax.ShapeDtypeStruct((ecoef, hidden_units), F32),
             jax.ShapeDtypeStruct((1, ecoef), F32),
         ),
-        in_specs=[vm()] * 8 + [sm(), vm()],
+        in_specs=[vm()] * 5 + [hbm(), hbm(), vm(), sm(), hbm()],
         out_specs=(vm(), vm(), vm(), vm(), vm()),
         scratch_shapes=scratch,
         compiler_params=pltpu.CompilerParams(
-            collective_id=0, has_side_effects=True, vmem_limit_bytes=48 * 1024 * 1024
+            collective_id=0, has_side_effects=True, vmem_limit_bytes=56 * 1024 * 1024
         ),
     )(picked, w_in, b_in[None], wt, bt, block_rows[0], loads[0], mask, elem_map[0], cotangent[0])
-    return (field[None], w_in_grad, b_in_grad[0], w_out_grad, b_out_grad[0])
+    field, w_in_grad, b_in_grad, w_out_grad, b_out_grad = pl.pallas_call(
+        write_out,
+        out_shape=tuple(jax.ShapeDtypeStruct(r.shape, r.dtype) for r in results),
+        in_specs=[hbm()] * 5,
+        out_specs=(hbm(),) * 5,
+        scratch_shapes=[dma((5,))],
+    )(*results)
+    return (field[None], w_in_grad, b_in_grad[0], w_out_grad.T, b_out_grad[0])
 
 
 def solution(mesh):

time: 74.1 us -> 103 us (1.39)
  Pallas kernels: 64.6 us -> 96.8 us
  local copies, waits for them, and re-layouts: 8.35 us -> 4.27 us
    pallas_call x0 -> x1, Pallas kernels: none -> 33.5 us  [local(): pl.pallas_call(write_out, out_shape=tuple((jax.ShapeDtypeStruct(r.shape,...]
    unnamed x25 -> x10, local copies, waits for them, and re-layouts: 7.06 us -> 2.13 us
    pallas_call x1, Pallas kernels: 64.6 us -> 63.3 us  [local(): pl.pallas_call(functools.partial(kernel, n_sx, n_sy), out_shape=(jax.Shap...]
where the time goes in v2:
time: 103 us; the launch traced here: 102 us
  Pallas kernels  96.8 us (94%)
  local copies, waits for them, and re-layouts  4.27 us (4%)
    pallas_call x1, Pallas kernels, local(): pl.pallas_call(functools.partial(kernel, n_sx, n_sy), out_shape=(jax.Shap...  63.3 us
    pallas_call x1, Pallas kernels, local(): pl.pallas_call(write_out, out_shape=tuple((jax.ShapeDtypeStruct(r.shape,...  33.5 us
    unnamed x10, local copies, waits for them, and re-layouts  2.13 us

profile of v2, /device:TPU:1, one launch (start us, length us, event | category | flops | bytes accessed | tf_op | source)
XLA Modules:
  0.0 102.5 jit_solution(17744644000181790300)
XLA Ops:
  0.6 0.0 copy-start
  0.6 0.7 copy-done
  1.3 0.0 copy-start.3
  1.3 0.7 copy-done.3
  2.0 0.0 copy-start.4
  2.0 0.0 copy-start.2
  2.0 0.1 broadcast_in_dim.27
  2.1 0.1 broadcast_in_dim.28
  2.2 0.5 copy-done.4
  2.7 0.1 tile.21
  2.8 0.5 pad_bitcast_fusion.b_out_ref
  3.3 0.0 copy-done.2
  3.3 0.7 copy.17
  4.0 0.0 copy-start.1
  4.0 0.7 concatenate.6.wt_ref
  4.6 0.3 copy-done.1
  4.9 0.7 bitcast_select_fusion.picked_ref
  5.7 63.3 %shard_map.146 = (f32[4,4,64,128]{3,2,1,0:T(8,128)}, f32[256,512]{1,0:T(8,128)}, f32[1,512]{1,0:T(1,128)}, f32[8,512]{1,0:T(8,128)}, f32[1,8]{1,0:T(1,128)}) custom-call(bf16[128,256]{1,0:T(8,128)(2,1)} %bitcast_select_fusion.picked_ref, bf16[256,512]{1,0:T(8,128)(2,1)} %w_in_ref.1, f32[1,512]{1,0:T(1,128)} %bitcast.28, bf16[128,512]{1,0:T(8,128)(2,1)} %concatenate.6.wt_ref, ...), custom_call_target="tpu_custom_call" | custom-call | tf_op jit(solution)/shard_map/pallas_call | solution.py:609
  69.0 33.5 %shard_map.147 = (f32[4,4,64,128]{3,2,1,0:T(8,128)}, f32[256,512]{1,0:T(8,128)}, f32[1,512]{1,0:T(1,128)}, f32[8,512]{1,0:T(8,128)}, f32[1,8]{1,0:T(1,128)}) custom-call(f32[4,4,64,128]{3,2,1,0:T(8,128)} %get-tuple-element.15.refs_0_, f32[256,512]{1,0:T(8,128)} %get-tuple-element.16.refs_1_, f32[1,512]{1,0:T(1,128)} %get-tuple-element.17.refs_2_, ...), custom_call_target="tpu_custom_call" | custom-call | tf_op jit(solution)/shard_map/pallas_call | solution.py:625
  (5 shorter events, 0.0 us)
Async XLA Ops:
  0.6 0.7 copy-start
  1.3 0.7 copy-start.3
  2.0 0.7 copy-start.4
  2.0 1.3 %copy-start.2 = (s32[1,4,4,64]{3,2,1,0:T(4,128)S(1)}, s32[1,4,4,64]{3,2,1,0:T(4,128)}, u32[]{:S(2)}) copy-start(s32[1,4,4,64]{3,2,1,0:T(4,128)} %param.19) | copy-start | bytes 12292
  4.0 1.0 copy-start.1

commit v3 on v2

--- a/solution.py
+++ b/solution.py
@@ -619,13 +619,13 @@
         out_specs=(vm(), vm(), vm(), vm(), vm()),
         scratch_shapes=scratch,
         compiler_params=pltpu.CompilerParams(
-            collective_id=0, has_side_effects=True, vmem_limit_bytes=56 * 1024 * 1024
+            collective_id=0, has_side_effects=True, vmem_limit_bytes=40 * 1024 * 1024
         ),
     )(picked, w_in, b_in[None], wt, bt, block_rows[0], loads[0], mask, elem_map[0], cotangent[0])
     field, w_in_grad, b_in_grad, w_out_grad, b_out_grad = pl.pallas_call(
         write_out,
         out_shape=tuple(jax.ShapeDtypeStruct(r.shape, r.dtype) for r in results),
-        in_specs=[hbm()] * 5,
+        in_specs=[vm()] * 5,
         out_specs=(hbm(),) * 5,
         scratch_shapes=[dma((5,))],
     )(*results)

time: 103 us -> 73.8 us (0.72)
  Pallas kernels: 96.8 us -> 64.3 us
  local copies, waits for them, and re-layouts: 4.27 us -> 8.29 us
    pallas_call x1, Pallas kernels: 33.5 us -> 2.23 us  [local(): pl.pallas_call(write_out, out_shape=tuple((jax.ShapeDtypeStruct(r.shape,...]
    unnamed x10 -> x30, local copies, waits for them, and re-layouts: 2.13 us -> 6.99 us
    pallas_call x1, Pallas kernels: 63.3 us -> 62.1 us  [local(): pl.pallas_call(functools.partial(kernel, n_sx, n_sy), out_shape=(jax.Shap...]
where the time goes in v3:
time: 73.8 us; the launch traced here: 73.4 us
  Pallas kernels  64.3 us (87%)
  local copies, waits for them, and re-layouts  8.29 us (11%)
  between operations  0.77 us (1%)
    pallas_call x1, Pallas kernels, local(): pl.pallas_call(functools.partial(kernel, n_sx, n_sy), out_shape=(jax.Shap...  62.1 us
    unnamed x30, local copies, waits for them, and re-layouts  6.99 us
    pallas_call x1, Pallas kernels, local(): pl.pallas_call(write_out, out_shape=tuple((jax.ShapeDtypeStruct(r.shape,...  2.23 us

profile of v3, /device:TPU:1, one launch (start us, length us, event | category | flops | bytes accessed | tf_op | source)
XLA Modules:
  0.0 73.4 jit_solution(4340899919778794197)
XLA Ops:
  0.6 0.0 copy-start
  0.6 0.7 copy-done
  1.3 0.0 copy-start.13
  1.3 0.7 copy-done.13
  2.0 0.0 copy-start.14
  2.0 0.0 copy-start.12
  2.0 0.1 broadcast_in_dim.27
  2.1 0.1 broadcast_in_dim.28
  2.2 0.5 copy-done.14
  2.7 0.1 tile.21
  2.8 0.0 copy-done.12
  2.8 0.0 copy-start.6
  2.8 0.1 copy.17
  2.9 0.0 copy-start.5
  2.9 0.0 copy-start.4
  2.9 0.9 %fusion = (bf16[1,4,4,1,8,256]{5,4,3,2,1,0:T(8,128)(2,1)S(1)}, bf16[1,4,4,1,8,256]{5,4,3,2,1,0:T(8,128)(2,1)S(1)}) fusion(bf16[1,4,4,2,8,256]{5,4,3,2,1,0:T(8,128)(2,1)} %param.11), kind=kLoop, calls=%fused_computation.4 | loop fusion | bytes 262144 | tf_op jit(solution)/shard_map/slice | solution.py:546
  3.9 0.0 copy-start.8
  3.9 0.0 copy-start.9
  3.9 0.1 bitcast_select_fusion.picked_ref
  4.0 0.0 copy-done.6
  4.0 0.0 copy-done.5
  4.0 0.0 copy-done.4
  4.0 0.6 copy-done.8
  4.6 0.0 copy-done.9
  4.6 0.0 copy-start.1
  4.6 1.2 %copy-done.1 = f32[1,4,4,64,256]{4,3,2,1,0:T(8,128)S(1)} copy-done((f32[1,4,4,64,256]{4,3,2,1,0:T(8,128)S(1)}, f32[1,4,4,64,256]{4,3,2,1,0:T(8,128)}, u32[]{:S(2)}) %copy-start.1) | copy-done | bytes 1048600
  5.8 62.1 %shard_map.146 = (f32[4,4,64,128]{3,2,1,0:T(8,128)S(1)}, f32[256,512]{1,0:T(8,128)S(1)}, f32[1,512]{1,0:T(1,128)S(1)}, f32[8,512]{1,0:T(8,128)S(1)}, f32[1,8]{1,0:T(1,128)S(1)}) custom-call(bf16[128,256]{1,0:T(8,128)(2,1)S(1)} %bitcast_select_fusion.picked_ref, bf16[256,512]{1,0:T(8,128)(2,1)S(1)} %copy-done.4, f32[1,512]{1,0:T(1,128)S(1)} %bitcast.27, ...), custom_call_target="tpu_custom_call" | custom-call | tf_op jit(solution)/shard_map/pallas_call | solution.py:609
  67.9 0.0 copy-start.2
  67.9 0.8 %copy-done.2 = f32[4,4,64,128]{3,2,1,0:T(8,128)} copy-done((f32[4,4,64,128]{3,2,1,0:T(8,128)}, f32[4,4,64,128]{3,2,1,0:T(8,128)S(1)}, u32[]{:S(2)}) %copy-start.2) | copy-done | bytes 524312
  68.7 0.0 copy-start.3
  68.7 0.8 %copy-done.3 = f32[256,512]{1,0:T(8,128)} copy-done((f32[256,512]{1,0:T(8,128)}, f32[256,512]{1,0:T(8,128)S(1)}, u32[]{:S(2)}) %copy-start.3) | copy-done | bytes 524312
  69.5 0.0 copy-start.7
  69.5 0.6 copy-done.7
  70.1 0.0 copy-start.11
  70.1 0.5 copy-done.11
  70.6 0.0 copy-start.10
  70.6 0.6 copy-done.10
  71.2 2.2 %shard_map.147 = (f32[4,4,64,128]{3,2,1,0:T(8,128)}, f32[256,512]{1,0:T(8,128)}, f32[1,512]{1,0:T(1,128)}, f32[8,512]{1,0:T(8,128)}, f32[1,8]{1,0:T(1,128)}) custom-call(f32[4,4,64,128]{3,2,1,0:T(8,128)} %copy-done.2, f32[256,512]{1,0:T(8,128)} %copy-done.3, f32[1,512]{1,0:T(1,128)} %copy-done.10, f32[8,512]{1,0:T(8,128)} %copy-done.7, f32[1,8]{1,0:T(1,128)} %copy-done.11), custom_call_target="tpu_custom_call" | custom-call | tf_op jit(solution)/shard_map/pallas_call | solution.py:625
  (6 shorter events, 0.0 us)
Async XLA Ops:
  0.6 0.7 copy-start
  1.3 0.7 copy-start.13
  2.0 0.7 copy-start.14
  2.0 0.7 %copy-start.12 = (s32[1,4,4,64]{3,2,1,0:T(4,128)S(1)}, s32[1,4,4,64]{3,2,1,0:T(4,128)}, u32[]{:S(2)}) copy-start(s32[1,4,4,64]{3,2,1,0:T(4,128)} %param.19) | copy-start | bytes 12292
  2.8 1.2 %copy-start.6 = (bf16[1,4,4,64,128]{4,3,2,1,0:T(8,128)(2,1)S(1)}, bf16[1,4,4,64,128]{4,3,2,1,0:T(8,128)(2,1)}, u32[]{:S(2)}) copy-start(bf16[1,4,4,64,128]{4,3,2,1,0:T(8,128)(2,1)} %param.21) | copy-start | bytes 786436
  2.9 1.1 %copy-start.5 = (bf16[1,4,4,64,128]{4,3,2,1,0:T(8,128)(2,1)S(1)}, bf16[1,4,4,64,128]{4,3,2,1,0:T(8,128)(2,1)}, u32[]{:S(2)}) copy-start(bf16[1,4,4,64,128]{4,3,2,1,0:T(8,128)(2,1)} %param.18) | copy-start | bytes 786436
  2.9 1.1 %copy-start.4 = (bf16[256,512]{1,0:T(8,128)(2,1)S(1)}, bf16[256,512]{1,0:T(8,128)(2,1)}, u32[]{:S(2)}) copy-start(bf16[256,512]{1,0:T(8,128)(2,1)} %w_in_ref.1) | copy-start | bytes 786436
  3.9 0.7 copy-start.8
  3.9 0.7 copy-start.9
  4.6 1.2 %copy-start.1 = (f32[1,4,4,64,256]{4,3,2,1,0:T(8,128)S(1)}, f32[1,4,4,64,256]{4,3,2,1,0:T(8,128)}, u32[]{:S(2)}) copy-start(f32[1,4,4,64,256]{4,3,2,1,0:T(8,128)} %param.17) | copy-start | bytes 3145732
  67.9 0.8 %copy-start.2 = (f32[4,4,64,128]{3,2,1,0:T(8,128)}, f32[4,4,64,128]{3,2,1,0:T(8,128)S(1)}, u32[]{:S(2)}) copy-start(f32[4,4,64,128]{3,2,1,0:T(8,128)S(1)} %get-tuple-element.15.refs_0_) | copy-start | bytes 1572868
  68.7 0.8 %copy-start.3 = (f32[256,512]{1,0:T(8,128)}, f32[256,512]{1,0:T(8,128)S(1)}, u32[]{:S(2)}) copy-start(f32[256,512]{1,0:T(8,128)S(1)} %get-tuple-element.16.refs_1_) | copy-start | bytes 1572868
  69.5 0.6 copy-start.7
  70.1 0.5 copy-start.11
  70.6 0.6 copy-start.10

commit v4 on v3

--- a/solution.py
+++ b/solution.py
@@ -521,15 +521,6 @@
         @pl.when(has_n)
         def _():
             face(3, r, 0).wait_send()
-
-
-def write_out(*refs):
-    sem = refs[-1]
-    copies = [pltpu.make_async_copy(refs[i], refs[i + 5], sem.at[i]) for i in range(5)]
-    for c in copies:
-        c.start()
-    for c in copies:
-        c.wait()
 
 
 def local(
@@ -622,13 +613,7 @@
             collective_id=0, has_side_effects=True, vmem_limit_bytes=40 * 1024 * 1024
         ),
     )(picked, w_in, b_in[None], wt, bt, block_rows[0], loads[0], mask, elem_map[0], cotangent[0])
-    field, w_in_grad, b_in_grad, w_out_grad, b_out_grad = pl.pallas_call(
-        write_out,
-        out_shape=tuple(jax.ShapeDtypeStruct(r.shape, r.dtype) for r in results),
-        in_specs=[vm()] * 5,
-        out_specs=(hbm(),) * 5,
-        scratch_shapes=[dma((5,))],
-    )(*results)
+    field, w_in_grad, b_in_grad, w_out_grad, b_out_grad = results
     return (field[None], w_in_grad, b_in_grad[0], w_out_grad.T, b_out_grad[0])
 
 

time: 73.8 us -> 71.5 us (0.969)
  Pallas kernels: 64.3 us -> 62.1 us
    pallas_call x1 -> x0, Pallas kernels: 2.23 us -> none  [local(): pl.pallas_call(write_out, out_shape=tuple((jax.ShapeDtypeStruct(r.shape,...]
    unnamed x30 -> x25, local copies, waits for them, and re-layouts: 6.99 us -> 6.96 us
where the time goes in v4:
time: 71.5 us; the launch traced here: 71.2 us
  Pallas kernels  62.1 us (87%)
  local copies, waits for them, and re-layouts  8.25 us (12%)
  between operations  0.76 us (1%)
    pallas_call x1, Pallas kernels, local(): pl.pallas_call(functools.partial(kernel, n_sx, n_sy), out_shape=(jax.Shap...  62.1 us
    unnamed x25, local copies, waits for them, and re-layouts  6.96 us

profile of v4, /device:TPU:1, one launch (start us, length us, event | category | flops | bytes accessed | tf_op | source)
XLA Modules:
  0.0 71.2 jit_solution(14960771843207175992)
XLA Ops:
  0.6 0.0 copy-start
  0.6 0.7 copy-done
  1.3 0.0 copy-start.8
  1.3 0.7 copy-done.8
  2.0 0.0 copy-start.9
  2.0 0.0 copy-start.7
  2.0 0.1 broadcast_in_dim.27
  2.1 0.1 broadcast_in_dim.28
  2.2 0.5 copy-done.9
  2.7 0.1 tile.21
  2.8 0.0 copy-done.7
  2.8 0.0 copy-start.4
  2.8 0.1 copy.17
  2.9 0.0 copy-start.3
  2.9 0.0 copy-start.2
  2.9 0.9 %fusion = (bf16[1,4,4,1,8,256]{5,4,3,2,1,0:T(8,128)(2,1)S(1)}, bf16[1,4,4,1,8,256]{5,4,3,2,1,0:T(8,128)(2,1)S(1)}) fusion(bf16[1,4,4,2,8,256]{5,4,3,2,1,0:T(8,128)(2,1)} %param.11), kind=kLoop, calls=%fused_computation.4 | loop fusion | bytes 262144 | tf_op jit(solution)/shard_map/slice | solution.py:537
  3.9 0.0 copy-start.5
  3.9 0.0 copy-start.6
  3.9 0.1 bitcast_select_fusion.picked_ref
  4.0 0.0 copy-done.4
  4.0 0.0 copy-done.3
  4.0 0.0 copy-done.2
  4.0 0.6 copy-done.5
  4.6 0.0 copy-done.6
  4.6 0.0 copy-start.1
  4.6 1.2 %copy-done.1 = f32[1,4,4,64,256]{4,3,2,1,0:T(8,128)S(1)} copy-done((f32[1,4,4,64,256]{4,3,2,1,0:T(8,128)S(1)}, f32[1,4,4,64,256]{4,3,2,1,0:T(8,128)}, u32[]{:S(2)}) %copy-start.1) | copy-done | bytes 1048600
  5.8 62.1 %shard_map.146 = (f32[4,4,64,128]{3,2,1,0:T(8,128)S(1)}, f32[256,512]{1,0:T(8,128)S(1)}, f32[1,512]{1,0:T(1,128)S(1)}, f32[8,512]{1,0:T(8,128)S(1)}, f32[1,8]{1,0:T(1,128)S(1)}) custom-call(bf16[128,256]{1,0:T(8,128)(2,1)S(1)} %bitcast_select_fusion.picked_ref, bf16[256,512]{1,0:T(8,128)(2,1)S(1)} %copy-done.2, f32[1,512]{1,0:T(1,128)S(1)} %bitcast.29, ...), custom_call_target="tpu_custom_call" | custom-call | tf_op jit(solution)/shard_map/pallas_call | solution.py:600
  67.9 0.8 %copy.23 = f32[1,4,4,64,128]{4,3,2,1,0:T(8,128)} copy(f32[1,4,4,64,128]{4,3,2,1,0:T(8,128)S(1)} %bitcast.24) | data formatting | bytes 1048576
  68.7 0.8 %copy.24 = f32[256,512]{1,0:T(8,128)} copy(f32[256,512]{1,0:T(8,128)S(1)} %get-tuple-element.23) | data formatting | bytes 1048576
  69.5 0.6 copy.25
  70.1 0.6 copy.26
  70.7 0.5 copy.27
  (6 shorter events, 0.0 us)
Async XLA Ops:
  0.6 0.7 copy-start
  1.3 0.7 copy-start.8
  2.0 0.7 copy-start.9
  2.0 0.7 %copy-start.7 = (s32[1,4,4,64]{3,2,1,0:T(4,128)S(1)}, s32[1,4,4,64]{3,2,1,0:T(4,128)}, u32[]{:S(2)}) copy-start(s32[1,4,4,64]{3,2,1,0:T(4,128)} %param.19) | copy-start | bytes 12292
  2.8 1.2 %copy-start.4 = (bf16[1,4,4,64,128]{4,3,2,1,0:T(8,128)(2,1)S(1)}, bf16[1,4,4,64,128]{4,3,2,1,0:T(8,128)(2,1)}, u32[]{:S(2)}) copy-start(bf16[1,4,4,64,128]{4,3,2,1,0:T(8,128)(2,1)} %param.21) | copy-start | bytes 786436
  2.9 1.1 %copy-start.3 = (bf16[1,4,4,64,128]{4,3,2,1,0:T(8,128)(2,1)S(1)}, bf16[1,4,4,64,128]{4,3,2,1,0:T(8,128)(2,1)}, u32[]{:S(2)}) copy-start(bf16[1,4,4,64,128]{4,3,2,1,0:T(8,128)(2,1)} %param.18) | copy-start | bytes 786436
  2.9 1.1 %copy-start.2 = (bf16[256,512]{1,0:T(8,128)(2,1)S(1)}, bf16[256,512]{1,0:T(8,128)(2,1)}, u32[]{:S(2)}) copy-start(bf16[256,512]{1,0:T(8,128)(2,1)} %w_in_ref.1) | copy-start | bytes 786436
  3.9 0.7 copy-start.5
  3.9 0.7 copy-start.6
  4.6 1.2 %copy-start.1 = (f32[1,4,4,64,256]{4,3,2,1,0:T(8,128)S(1)}, f32[1,4,4,64,256]{4,3,2,1,0:T(8,128)}, u32[]{:S(2)}) copy-start(f32[1,4,4,64,256]{4,3,2,1,0:T(8,128)} %param.17) | copy-start | bytes 3145732
